TPU v7x, 512 devices: a whole 4x4x16 slice. The times are simulated.
512 devices in a mesh: dp: 4 (over z_hi), tensor: 8 (over x, core), pre: 16 (over z_lo, y).
Axes of the slice: x: 4, y: 4, z: 16 (z_hi: 4, z_lo: 4; z = z_hi * 4 + z_lo), core: 2. Of those that a mesh axis runs over, the one named last changes fastest.
Arguments:
- grad_parts: bfloat16 [4, 32, 1024, 1024], P('dp', None, 'pre', 'tensor'), may hold values from -1.25 to 1.25
- slot_block: int32 [32], replicated, may hold values from 0 to 31, each once
- left_factor: float32 [32, 1024, 1024], P(('dp', 'tensor'), 'pre'), may hold values from -6 to 6
- right_factor: float32 [32, 1024, 1024], P(('dp', 'tensor'), 'pre'), may hold values from -6 to 6
- first_moment: float32 [32, 1024, 1024], P(('dp', 'tensor'), 'pre'), may hold values from -0.75 to 0.75
- second_moment: float32 [32, 1024, 1024], P(('dp', 'tensor'), 'pre'), may hold values from 0.001 to 0.01
- left_basis: bfloat16 [32, 1024, 1024], P(('dp', 'tensor'), 'pre'), may hold values from -0.1875 to 0.1875
- right_basis: bfloat16 [32, 1024, 1024], P(('dp', 'tensor'), 'pre'), may hold values from -0.1875 to 0.1875
- weight: bfloat16 [32, 1024, 1024], P(None, 'pre', 'tensor'), may hold values from -6 to 6
Outputs:
- new_left: float32 [32, 1024, 1024], P(('dp', 'tensor'), 'pre')
- new_right: float32 [32, 1024, 1024], P(('dp', 'tensor'), 'pre')
- new_first: float32 [32, 1024, 1024], P(('dp', 'tensor'), 'pre')
- new_second: float32 [32, 1024, 1024], P(('dp', 'tensor'), 'pre')
- update: bfloat16 [32, 1024, 1024], P(None, 'pre', 'tensor')
Inputs may be any that keep to these rules, and one draw needn't show every extreme that they name: `slot_block`: each block is named by exactly one owner.
All inputs are finite; a program needn't handle non-finite values.
Results may differ from a plain program's by a relative error of at most 0.02.
Values may be sent and summed in bfloat16 or wider, within the bound.
A program may use at most 64 MiB of HBM per device.

v0:
```python
import jax
import jax.numpy as jnp
from jax import lax
from jax.sharding import PartitionSpec as P

factor_decay = 0.95
first_decay = 0.95
second_decay = 0.95
first_fix = 1.0 - (0.95**10) ** 10
second_fix = 1.0 - (0.95**10) ** 10
epsilon = 1e-08
weight_decay = 0.1


def local(
    grad_parts,
    slot_block,
    left_factor,
    right_factor,
    first_moment,
    second_moment,
    left_basis,
    right_basis,
    weight,
):
    count_dp = lax.axis_size("dp")
    count_tensor = lax.axis_size("tensor")
    local_parts = grad_parts[0]
    nblocks, height, narrow = local_parts.shape
    ordered = jnp.take(local_parts, slot_block, axis=0)
    shares = lax.psum_scatter(
        ordered.astype(jnp.float32).astype(jnp.bfloat16), "dp", scatter_dimension=1, tiled=True
    )
    arrived = lax.all_to_all(shares, ("dp", "tensor"), split_axis=0, concat_axis=0, tiled=True)
    quarter = height // count_dp
    arrived = arrived.reshape(count_dp, count_tensor, quarter, narrow)
    gradient = jnp.transpose(arrived, (0, 2, 1, 3)).reshape(height, count_tensor * narrow)
    own_start = lax.axis_index("pre") * height
    leading = (((0,), (0,)), ((), ()))
    trailing = (((1,), (1,)), ((), ()))
    grad_portion = lax.all_gather(gradient, "pre", axis=0, tiled=True)
    basis_portion = lax.all_gather(left_basis[0], "pre", axis=0, tiled=True)
    block_left = lax.dot_general(
        gradient, grad_portion, trailing, preferred_element_type=jnp.float32
    )
    gram_left = block_left
    grad_cols = lax.dynamic_slice_in_dim(grad_portion, own_start, height, 1)
    basis_cols = lax.dynamic_slice_in_dim(basis_portion, own_start, height, 1)
    gram_right = lax.dot_general(
        grad_cols, grad_portion, leading, preferred_element_type=jnp.float32
    )
    projected = lax.dot_general(
        basis_cols, grad_portion, leading, preferred_element_type=jnp.float32
    )
    gram_left, gram_right, projected = (gram_left, gram_right, projected)
    left_next = factor_decay * left_factor[0] + (1.0 - factor_decay) * gram_left
    right_next = factor_decay * right_factor[0] + (1.0 - factor_decay) * gram_right
    right_whole = lax.all_gather(right_basis[0], "pre", axis=0, tiled=True)
    rotated = jnp.dot(
        projected.astype(jnp.bfloat16), right_whole, preferred_element_type=jnp.float32
    )
    first_next = first_decay * first_moment[0] + (1.0 - first_decay) * rotated
    second_next = second_decay * second_moment[0] + (1.0 - second_decay) * rotated * rotated
    direction = (first_next / first_fix / (jnp.sqrt(second_next / second_fix) + epsilon)).astype(
        jnp.bfloat16
    )
    counter = lax.dot_general(
        direction, right_whole, trailing, preferred_element_type=jnp.float32
    ).astype(jnp.bfloat16)
    basis_own = left_basis[0]
    unrotated = jnp.dot(
        basis_own,
        lax.all_gather(counter, "pre", axis=0, tiled=True),
        preferred_element_type=jnp.float32,
    ).astype(jnp.bfloat16)
    split_cols = unrotated.reshape(height, count_tensor, narrow)
    landed = lax.all_to_all(split_cols, "tensor", split_axis=1, concat_axis=0, tiled=True).reshape(
        count_tensor, height, narrow
    )
    landed = lax.all_gather(landed, "dp", axis=0, tiled=True)
    numbers = jnp.arange(nblocks, dtype=jnp.int32)
    inverse = jnp.sum(
        jnp.where(slot_block[None, :] == numbers[:, None], numbers[None, :], 0), axis=1
    )
    blocks = jnp.take(landed, inverse, axis=0)
    update = (blocks.astype(jnp.float32) + weight_decay * weight.astype(jnp.float32)).astype(
        jnp.bfloat16
    )
    return (left_next[None], right_next[None], first_next[None], second_next[None], update)


def solution(mesh):
    return jax.shard_map(
        local,
        mesh=mesh,
        in_specs=(
            P("dp", None, "pre", "tensor"),
            P(),
            P(("dp", "tensor"), "pre", None),
            P(("dp", "tensor"), "pre", None),
            P(("dp", "tensor"), "pre", None),
            P(("dp", "tensor"), "pre", None),
            P(("dp", "tensor"), "pre", None),
            P(("dp", "tensor"), "pre", None),
            P(None, "pre", "tensor"),
        ),
        out_specs=(
            P(("dp", "tensor"), "pre", None),
            P(("dp", "tensor"), "pre", None),
            P(("dp", "tensor"), "pre", None),
            P(("dp", "tensor"), "pre", None),
            P(None, "pre", "tensor"),
        ),
        check_vma=False,
    )
```

profile of v0, /device:TPU:8, one launch (start us, length us, event | category | flops | bytes accessed | tf_op | source)
XLA Modules:
  0.0 438.0 jit_solution(8563037122832614867)
XLA Ops:
  8.0 0.0 reduce-scatter.2.cloned.1.call-start
  8.1 0.7 compare_select_fusion.1
  8.8 0.7 compare_and_fusion.1
  9.4 0.6 gather_fusion
  10.1 0.9 broadcast_select_fusion
  11.0 0.0 all-gather.14.cloned.1.call-start
  11.1 0.5 all-gather.14.cloned.1.call-update
  11.6 0.0 all-gather.12.cloned.1.call-start
  11.7 0.5 all-gather.12.cloned.1.call-update
  12.2 0.0 all-gather.8.cloned.1.call-start
  12.3 49.3 %reduce-scatter.2.cloned.1.call-done = bf16[32,16,128]{2,1,0:T(8,128)(2,1)} async-done(((bf16[32,64,128]{2,1,0:T(8,128)(2,1)}), bf16[32,16,128]{2,1,0:T(8,128)(2,1)}) %reduce-scatter.2.cloned.1.call-update) | async-done | bytes 131088 | tf_op jit(solution)/shard_map/reduce_scatter | solution.py:31
  61.6 24.3 %all_to_all.20 = bf16[32,16,128]{2,1,0:T(8,128)(2,1)S(1)} all-to-all(bf16[32,16,128]{2,1,0:T(8,128)(2,1)} %reduce-scatter.2.cloned.1.call-done), channel_id=1, replica_groups=mesh['dp'=4,'tensor'=8,'pre'=16] {'dp','tensor'}, dimensions={0} | all-to-all | bytes 262144 | tf_op jit(solution)/shard_map/all_to_all | solution.py:34
  85.9 0.7 copy.25
  86.6 0.0 all-gather.10.cloned.1.call-start
  86.7 28.3 %all-gather.14.cloned.1.call-done = bf16[1,1024,1024]{2,1,0:T(8,128)(2,1)} async-done(((bf16[1,64,1024]{2,1,0:T(8,128)(2,1)}), bf16[1,1024,1024]{2,1,0:T(8,128)(2,1)}) %all-gather.14.cloned.1.call-update) | async-done | bytes 2097168 | tf_op jit(solution)/shard_map/all_gather | solution.py:58
  115.0 90.3 %all-gather.12.cloned.1.call-done = bf16[1,1024,1024]{2,1,0:T(8,128)(2,1)} async-done(((bf16[1,64,1024]{2,1,0:T(8,128)(2,1)}), bf16[1,1024,1024]{2,1,0:T(8,128)(2,1)}) %all-gather.12.cloned.1.call-update) | async-done | bytes 2097168 | tf_op jit(solution)/shard_map/all_gather | solution.py:42
  205.4 89.4 %all-gather.8.cloned.1.call-done = bf16[1024,1024]{1,0:T(8,128)(2,1)} async-done(((bf16[64,1024]{1,0:T(8,128)(2,1)}), bf16[1024,1024]{1,0:T(8,128)(2,1)}) %all-gather.8.cloned.1.call-update) | async-done | bytes 2097168 | tf_op jit(solution)/shard_map/all_gather | solution.py:41
  294.8 3.3 fusion.2
  298.1 3.2 fusion.8
  301.3 0.0 all-gather.10.cloned.1.call-update
  301.4 0.1 select_reduce_fusion
  301.5 2.4 fusion.7
  303.9 0.9 fusion.23
  304.8 83.5 %all-gather.10.cloned.1.call-done = bf16[1024,1024]{1,0:T(8,128)(2,1)} async-done(((bf16[64,1024]{1,0:T(8,128)(2,1)}), bf16[1024,1024]{1,0:T(8,128)(2,1)}) %all-gather.10.cloned.1.call-update) | async-done | bytes 2097168 | tf_op jit(solution)/shard_map/all_gather | solution.py:73
  388.3 2.1 fusion.11
  390.5 0.7 copy.26
  391.2 4.3 all-to-all-start.1
  395.5 2.3 fusion.5
  397.8 3.8 all-to-all-done.1
  401.6 27.1 %all-gather.2 = bf16[32,64,1,128]{3,1,2,0:T(8,128)(2,1)S(1)} all-gather(bf16[8,64,1,128]{3,1,2,0:T(8,128)(2,1)S(1)} %bitcast.67), channel_id=4, replica_groups=mesh['dp'=4,'tensor'=8,'pre'=16] {'dp'}, dimensions={0}, use_global_device_ids=true | all-gather | bytes 655360 | tf_op jit(solution)/shard_map/all_gather | solution.py:80
  428.7 0.6 gather_fusion.1
  429.4 1.0 add_convert_fusion
  (19 shorter events, 0.1 us)
Async XLA Ops:
  8.0 1.4 copy-start
  8.0 53.5 %reduce-scatter.2.cloned.1.call-start = ((), (), s32[]{:S(2)}) async-start(), calls=%async_computation.3 | async-start | bytes 655360 | tf_op jit(solution)/shard_map/reduce_scatter | solution.py:31
  11.0 104.0 %all-gather.14.cloned.1.call-start = ((), (), s32[]{:S(2)}) async-start(), calls=%async_computation.7 | async-start | bytes 2228224 | tf_op jit(solution)/shard_map/all_gather | solution.py:58
  11.6 193.7 %all-gather.12.cloned.1.call-start = ((), (), s32[]{:S(2)}) async-start(), calls=%async_computation.6 | async-start | bytes 2228224 | tf_op jit(solution)/shard_map/all_gather | solution.py:42
  12.2 282.6 %all-gather.8.cloned.1.call-start = ((), (), s32[]{:S(2)}) async-start(), calls=%async_computation.4 | async-start | bytes 2228224 | tf_op jit(solution)/shard_map/all_gather | solution.py:41
  86.6 301.7 %all-gather.10.cloned.1.call-start = ((), (), s32[]{:S(2)}) async-start(), calls=%async_computation.5 | async-start | bytes 2228224 | tf_op jit(solution)/shard_map/all_gather | solution.py:73
  86.7 211.4 %copy-start.2 = (f32[1,64,1024]{2,1,0:T(8,128)S(1)}, f32[1,64,1024]{2,1,0:T(8,128)}, u32[]{:S(2)}) copy-start(f32[1,64,1024]{2,1,0:T(8,128)} %param.16) | copy-start | bytes 786436
  86.7 211.4 %copy-start.3 = (f32[1,64,1024]{2,1,0:T(8,128)S(1)}, f32[1,64,1024]{2,1,0:T(8,128)}, u32[]{:S(2)}) copy-start(f32[1,64,1024]{2,1,0:T(8,128)} %param.15) | copy-start | bytes 786436
  298.1 3.2 copy-start.5
  298.1 3.4 copy-start.1
  391.2 10.4 %all-to-all-start.1 = ((bf16[64,8,128]{2,0,1:T(8,128)(2,1)}), bf16[64,8,128]{2,0,1:T(8,128)(2,1)S(1)}, u32[]{:S(2)}, u32[]{:S(2)}) async-start(bf16[64,8,128]{2,0,1:T(8,128)(2,1)} %bitcast.62), calls=%async_computation.2 | async-start | bytes 262144 | tf_op jit(solution)/shard_map/all_to_all | solution.py:77
  395.5 33.9 %copy-start.4 = (bf16[32,64,128]{2,1,0:T(8,128)(2,1)S(1)}, bf16[32,64,128]{2,1,0:T(8,128)(2,1)}, u32[]{:S(2)}) copy-start(bf16[32,64,128]{2,1,0:T(8,128)(2,1)} %param.19) | copy-start | bytes 1572868
Sparse Core Ops, SparseCore 0:
  12.2 49.2 reduce-scatter.1
Sparse Core Ops, SparseCore 1:
  13.6 101.4 all-gather.13
  117.0 88.3 all-gather.11
  207.9 86.8 all-gather.7
  301.4 86.8 all-gather.9
where the time goes:
time: 438 us
  waiting for transfers between devices  346 us (79%)
  blocking collectives  51.4 us (12%)
  between operations  15.8 us (4%)
  matrix products  13.4 us (3%)
  starting transfers between devices  4.51 us (1%)
    all_gather x1, waiting for transfers between devices, local(): basis_portion = lax.all_gather(left_basis[0], 'pre', axis=0, tiled=True)  90.3 us
    all_gather x1, waiting for transfers between devices, local(): grad_portion = lax.all_gather(gradient, 'pre', axis=0, tiled=True)  89.4 us
    all_gather x1, waiting for transfers between devices, local(): lax.all_gather(counter, 'pre', axis=0, tiled=True)  83.5 us
    reduce_scatter x1, waiting for transfers between devices, local(): lax.psum_scatter(ordered.astype(jnp.float32).astype(jnp.bfloat16), 'dp',...  49.3 us
    all_gather x1, waiting for transfers between devices, local(): right_whole = lax.all_gather(right_basis[0], 'pre', axis=0, tiled=True)  28.3 us
    all_gather x1, blocking collectives, local(): landed = lax.all_gather(landed, 'dp', axis=0, tiled=True)  27.1 us
    all_to_all x1, blocking collectives, local(): lax.all_to_all(shares, ('dp', 'tensor'), split_axis=0, concat_axis=0, til...  24.3 us
  transfers between devices with their start and end apart: 6, of which 6 were waited for; matrix products, arithmetic and copies ran while one was open for 1% of the time, Pallas kernels for 0%

commit v1 on v0

v1 whole, which is shorter than its diff:
```python
import jax
import jax.numpy as jnp
from jax import lax
from jax.experimental import pallas as pl
from jax.experimental.pallas import tpu as pltpu
from jax.sharding import PartitionSpec as P

factor_decay = 0.95
first_decay = 0.95
second_decay = 0.95
first_fix = 1.0 - (0.95**10) ** 10
second_fix = 1.0 - (0.95**10) ** 10
epsilon = 1e-08
weight_decay = 0.1

MESH = pl.DeviceIdType.MESH
F32 = jnp.float32
BF16 = jnp.bfloat16


def towards(zl, plane, parity):
    key = 2 * (zl - plane) + 2 * parity - 1
    return 2 * ((key + 16) // 16) - 1


def dot(a, b, dims=((1,), (0,))):
    return lax.dot_general(a, b, (dims, ((), ())), preferred_element_type=F32)


def kernel(
    slot, grad, left_old, right_old, first_old, second_old, basis_left, basis_right, weight,
    left_new, right_new, first_new, second_new, update,
    stage, rin, acc, gin, ghalf, qlh, qr, gfull, gturn, psend, precv, pfull, prow, rot, cbuf, cnt, unrot, land, inv,
    s1s, s1r, s2s, s2r, lzs, lzr, lys, lyr, rzs, rzr, rys, ryr, gzs, gzr, gys, gyr,
    pxs, pxr, prs, prr, cs, cr_, cxs, cxr, us, uf, ur,
):
    k, t, p = lax.axis_index("dp"), lax.axis_index("tensor"), lax.axis_index("pre")
    x, co, zl, y = t // 2, t % 2, p // 4, p % 4
    half = zl // 2
    tr = (zl % 2) * 4 + y
    up, down = (y + 1) % 4, (y + 3) % 4
    sent = []

    def push(src, dst, ssem, rsem, dev, here=None):
        copy = pltpu.make_async_remote_copy(
            src_ref=src, dst_ref=dst, send_sem=ssem, recv_sem=rsem, device_id=dev, device_id_type=MESH
        )
        if here is None:
            copy.start()
            sent.append((copy, None))
        else:
            away = jnp.logical_not(here)
            pl.when(away)(copy.start)
            pl.when(here)(pltpu.make_async_copy(src, dst, rsem).start)
            sent.append((copy, away))

    def arrived(dst, rsem):
        pltpu.make_async_copy(dst, dst, rsem).wait()

    for o in range(32):
        stage[(o // 8) * 8 + (o % 2) * 4 + (o % 8) // 2] = grad[slot[o]]
    signs = [towards(zl, 2 * c + t // 4, t % 2) for c in range(2)]
    for c in range(2):
        s = signs[c]
        d1, d2 = (k - s + 4) % 4, (k + 2) % 4
        push(stage.at[pl.ds(d1 * 8 + c * 4, 4)], rin.at[c, 0], s1s.at[c * 2], s1r.at[c * 2], (d1, t, p))
        push(
            stage.at[pl.ds(d2 * 8 + c * 4, 4)], rin.at[c, 1], s1s.at[c * 2 + 1], s1r.at[c * 2 + 1],
            ((k + s + 4) % 4, t, p),
        )

    for j in range(2):
        push(
            basis_left, qlh.at[pl.ds((p % 8) * 64, 64)], lzs.at[j], lzr.at[zl % 2],
            (k, x * 2 + half, (2 * co + j) * 4 + y),
            here=jnp.logical_and(half == co, zl % 2 == j),
        )
    own_rows = pl.ds(p * 64, 64)
    pltpu.make_async_copy(basis_right, qr.at[own_rows], rzr.at[zl]).start()
    for i in range(1, 4):
        push(basis_right, qr.at[own_rows], rzs.at[i - 1], rzr.at[zl], (k, t, ((zl + i) % 4) * 4 + y))

    slots = [slot[o] for o in range(32)]

    def invert(b, carry):
        total = jnp.int32(0)
        for o in range(32):
            place = (o // 8) * 8 + (o % 2) * 4 + (o % 8) // 2
            total = jnp.where(slots[o] == b, jnp.int32(place), total)
        inv[b] = total
        return carry

    lax.fori_loop(0, 32, invert, 0)

    def lrows(j, yy):
        return qlh.at[pl.ds((j * 4 + yy) * 64, 64)]

    for j in range(2):
        arrived(lrows(j, y), lzr.at[j])
        push(lrows(j, y), lrows(j, y), lys.at[j * 3], lyr.at[j * 3], (k, t, zl * 4 + up))
        push(lrows(j, y), lrows(j, y), lys.at[j * 3 + 1], lyr.at[j * 3 + 1], (k, t, zl * 4 + down))

    for c in range(2):
        s = signs[c]
        for way in range(2):
            arrived(rin.at[c, way], s1r.at[c * 2 + way])
            owner = k if way == 0 else (k + s + 4) % 4
            mine = stage[pl.ds(owner * 8 + c * 4, 4)]
            acc[c, way] = (mine.astype(F32) + rin[c, way].astype(F32)).astype(BF16)
            for xx in range(4):
                place = (owner, xx * 2 + half, (2 * c + t // 4) * 4 + t % 4)
                here = None
                if way == 0:
                    here = (xx * 2 + half == t) & (2 * c + t // 4 == zl) & (t % 4 == y)
                push(
                    acc.at[c, way, xx], gin.at[way, p % 8], s2s.at[c * 8 + way * 4 + xx], s2r.at[way * 8 + p % 8],
                    place, here,
                )

    arrived(lrows(0, down), lyr.at[0])
    push(lrows(0, down), lrows(0, down), lys.at[2], lyr.at[2], (k, t, zl * 4 + up))
    arrived(lrows(1, up), lyr.at[4])
    push(lrows(1, up), lrows(1, up), lys.at[5], lyr.at[5], (k, t, zl * 4 + down))

    def rrows(j, yy):
        return qr.at[pl.ds((j * 4 + yy) * 64, 64)]

    for j in range(4):
        arrived(rrows(j, y), rzr.at[j])
        push(rrows(j, y), rrows(j, y), rys.at[j * 3], ryr.at[j * 3], (k, t, zl * 4 + up))
        push(rrows(j, y), rrows(j, y), rys.at[j * 3 + 1], ryr.at[j * 3 + 1], (k, t, zl * 4 + down))

    for q in range(8):
        for way in range(2):
            arrived(gin.at[way, q], s2r.at[way * 8 + q])
        ghalf[pl.ds(q * 64, 64)] = (gin[0, q].astype(F32) + gin[1, q].astype(F32)).astype(BF16)

    arrived(lrows(1, down), lyr.at[3])
    arrived(lrows(0, up), lyr.at[1])
    opposite = (y + 2) % 4
    arrived(lrows(0, opposite), lyr.at[2])
    arrived(lrows(1, opposite), lyr.at[5])

    for n in range(2):
        lanes = pl.ds(pl.multiple_of((1 - co) * 512 + n * 256, 256), 256)
        psend[pl.ds(n * 256, 256)] = dot(qlh[:, lanes], ghalf[...], ((0,), (0,))).astype(BF16)
    push(psend, precv, pxs, pxr, (k, x * 2 + 1 - co, p))
    for j in range(4):
        push(
            ghalf, gfull.at[pl.ds(co * 512, 512), pl.ds(pl.multiple_of(tr * 128, 128), 128)],
            gzs.at[j], gzr.at[(zl % 2) * 2 + co], (k, x * 2 + half, j * 4 + y),
            here=(half == co) & (zl == j),
        )
    parts = []
    for n in range(2):
        lanes = pl.ds(pl.multiple_of(co * 512 + n * 256, 256), 256)
        parts.append(dot(qlh[:, lanes], ghalf[...], ((0,), (0,))))
    arrived(precv, pxr)
    for n in range(2):
        rows = pl.ds(n * 256, 256)
        pfull[rows] = (parts[n] + precv[rows].astype(F32)).astype(BF16)
    for q in range(8):
        push(
            pfull.at[pl.ds(q * 64, 64)], prow.at[:, pl.ds(pl.multiple_of(tr * 128, 128), 128)], prs.at[q], prr.at[tr],
            (k, x * 2 + half, co * 8 + q), here=(half == co) & (co * 8 + q == p),
        )

    for j in range(4):
        if j < 2:
            arrived(rrows(j, down), ryr.at[j * 3])
            push(rrows(j, down), rrows(j, down), rys.at[j * 3 + 2], ryr.at[j * 3 + 2], (k, t, zl * 4 + up))
        else:
            arrived(rrows(j, up), ryr.at[j * 3 + 1])
            push(rrows(j, up), rrows(j, up), rys.at[j * 3 + 2], ryr.at[j * 3 + 2], (k, t, zl * 4 + down))
    for j in range(4):
        if j < 2:
            arrived(rrows(j, up), ryr.at[j * 3 + 1])
        else:
            arrived(rrows(j, down), ryr.at[j * 3])
        arrived(rrows(j, opposite), ryr.at[j * 3 + 2])

    for tt in range(8):
        arrived(prow.at[:, pl.ds(tt * 128, 128)], prr.at[tt])
    for n in range(4):
        lanes = pl.ds(n * 256, 256)
        rotated = dot(prow[...], qr[:, lanes])
        first_next = first_decay * first_old[:, lanes] + (1.0 - first_decay) * rotated
        second_next = second_decay * second_old[:, lanes] + (1.0 - second_decay) * rotated * rotated
        first_new[:, lanes] = first_next
        second_new[:, lanes] = second_next
        rot[:, lanes] = (first_next / first_fix / (jnp.sqrt(second_next / second_fix) + epsilon)).astype(BF16)
    for n in range(4):
        cbuf[:, pl.ds(n * 256, 256)] = dot(rot[...], qr[pl.ds(n * 256, 256), :], ((1,), (1,))).astype(BF16)
        for tt in (2 * n, 2 * n + 1):
            push(
                cbuf.at[:, pl.ds(tt * 128, 128)], cnt.at[own_rows], cs.at[tt], cr_.at[p % 8],
                (k, x * 2 + half, (2 * co + tt // 4) * 4 + tt % 4), here=(half == co) & (tr == tt),
            )

    def gpart(tt, hh, yy):
        return gfull.at[pl.ds(hh * 512, 512), pl.ds(pl.multiple_of((tt * 4 + yy) * 128, 128), 128)]

    def gather_first(j):
        tt, hh = j // 2, j % 2
        arrived(gpart(tt, hh, y), gzr.at[j])
        push(gpart(tt, hh, y), gpart(tt, hh, y), gys.at[j * 3], gyr.at[j * 3], (k, t, zl * 4 + up))
        push(gpart(tt, hh, y), gpart(tt, hh, y), gys.at[j * 3 + 1], gyr.at[j * 3 + 1], (k, t, zl * 4 + down))

    def gather_relay(j):
        tt, hh = j // 2, j % 2
        if tt == 0:
            arrived(gpart(tt, hh, down), gyr.at[j * 3])
            push(gpart(tt, hh, down), gpart(tt, hh, down), gys.at[j * 3 + 2], gyr.at[j * 3 + 2], (k, t, zl * 4 + up))
        else:
            arrived(gpart(tt, hh, up), gyr.at[j * 3 + 1])
            push(gpart(tt, hh, up), gpart(tt, hh, up), gys.at[j * 3 + 2], gyr.at[j * 3 + 2], (k, t, zl * 4 + down))

    def gather_last(j):
        tt, hh = j // 2, j % 2
        if tt == 0:
            arrived(gpart(tt, hh, up), gyr.at[j * 3 + 1])
        else:
            arrived(gpart(tt, hh, down), gyr.at[j * 3])
        arrived(gpart(tt, hh, opposite), gyr.at[j * 3 + 2])

    for j in range(4):
        gather_first(j)

    def crows(hh, q):
        return cnt.at[pl.ds((hh * 8 + q) * 64, 64)]

    for q in range(8):
        arrived(crows(co, q), cr_.at[q])
        push(crows(co, q), crows(co, q), cxs.at[q], cxr.at[q], (k, x * 2 + 1 - co, p))
    for q in range(8):
        arrived(crows(1 - co, q), cxr.at[q])
    for n in range(2):
        unrot[pl.ds(n * 256, 256)] = dot(qlh[pl.ds(n * 256, 256), :], cnt[...]).astype(BF16)
        for q in range(n * 4, n * 4 + 4):
            s = towards(2 * co + q // 4, zl, tr % 2)
            index = k * 8 + half * 4 + x
            there = co * 8 + q
            push(
                unrot.at[pl.ds(q * 64, 64)], land.at[index], us.at[q * 2], ur.at[index], (k, tr, there),
                here=(tr == t) & (there == p),
            )
            push(
                unrot.at[pl.ds(q * 64, 64)], land.at[index], us.at[q * 2 + 1], ur.at[index],
                ((k - s + 4) % 4, tr, there),
            )

    for j in range(4):
        gather_relay(j)

    for c in range(2):
        s = signs[c]
        for xx in range(4):
            one, two = k * 8 + c * 4 + xx, ((k + s + 4) % 4) * 8 + c * 4 + xx
            arrived(land.at[one], ur.at[one])
            push(land.at[one], land.at[one], uf.at[c * 8 + xx], ur.at[one], ((k + s + 4) % 4, t, p))
            arrived(land.at[two], ur.at[two])
            push(land.at[two], land.at[two], uf.at[c * 8 + 4 + xx], ur.at[two], ((k - s + 4) % 4, t, p))

    for j in range(4):
        gather_last(j)
    gcols = gfull[:, pl.ds(pl.multiple_of((p // 2) * 128, 128), 128)]
    gturn[...] = gcols.astype(F32).T.astype(BF16)
    for n in range(4):
        lanes = pl.ds(n * 256, 256)
        left_new[:, lanes] = factor_decay * left_old[:, lanes] + (1.0 - factor_decay) * dot(
            gfull[own_rows, :], gfull[lanes, :], ((1,), (1,))
        )
    for n in range(4):
        lanes = pl.ds(n * 256, 256)
        right_new[:, lanes] = factor_decay * right_old[:, lanes] + (1.0 - factor_decay) * dot(
            gturn[pl.ds((p % 2) * 64, 64), :], gfull[:, lanes]
        )

    for c in range(2):
        s = signs[c]
        for xx in range(4):
            three, four = ((k - s + 4) % 4) * 8 + c * 4 + xx, ((k + 2) % 4) * 8 + c * 4 + xx
            arrived(land.at[three], ur.at[three])
            arrived(land.at[four], ur.at[four])

    for b in range(32):
        update[b] = (land[inv[b]].astype(F32) + weight_decay * weight[b].astype(F32)).astype(BF16)

    for copy, away in sent:
        if away is None:
            copy.wait_send()
        else:
            pl.when(away)(copy.wait_send)


def local(
    grad_parts, slot_block, left_factor, right_factor, first_moment, second_moment, left_basis, right_basis, weight
):
    vmem = pl.BlockSpec(memory_space=pltpu.VMEM)
    dma = lambda n: pltpu.SemaphoreType.DMA((n,))
    one = pltpu.SemaphoreType.DMA
    factor = jax.ShapeDtypeStruct((64, 1024), F32)
    outs = pl.pallas_call(
        kernel,
        out_shape=[factor] * 4 + [jax.ShapeDtypeStruct((32, 64, 128), BF16)],
        in_specs=[pl.BlockSpec(memory_space=pltpu.SMEM)] + [vmem] * 8,
        out_specs=[vmem] * 5,
        scratch_shapes=[
            pltpu.VMEM((32, 64, 128), BF16),
            pltpu.VMEM((2, 2, 4, 64, 128), BF16),
            pltpu.VMEM((2, 2, 4, 64, 128), BF16),
            pltpu.VMEM((2, 8, 64, 128), BF16),
            pltpu.VMEM((512, 128), BF16),
            pltpu.VMEM((512, 1024), BF16),
            pltpu.VMEM((1024, 1024), BF16),
            pltpu.VMEM((1024, 1024), BF16),
            pltpu.VMEM((128, 1024), BF16),
            pltpu.VMEM((512, 128), BF16),
            pltpu.VMEM((512, 128), BF16),
            pltpu.VMEM((512, 128), BF16),
            pltpu.VMEM((64, 1024), BF16),
            pltpu.VMEM((64, 1024), BF16),
            pltpu.VMEM((64, 1024), BF16),
            pltpu.VMEM((1024, 128), BF16),
            pltpu.VMEM((512, 128), BF16),
            pltpu.VMEM((32, 64, 128), BF16),
            pltpu.SMEM((32,), jnp.int32),
            dma(4), dma(4), dma(16), dma(16),
            dma(2), dma(2), dma(6), dma(6),
            dma(3), dma(4), dma(12), dma(12),
            dma(4), dma(4), dma(12), dma(12),
            one, one, dma(8), dma(8),
            dma(8), dma(8), dma(8), dma(8),
            dma(16), dma(16), dma(32),
        ],
        compiler_params=pltpu.CompilerParams(has_side_effects=True, vmem_limit_bytes=40 * 1024 * 1024),
        name="soap",
    )(
        slot_block, grad_parts[0], left_factor[0], right_factor[0], first_moment[0], second_moment[0],
        left_basis[0], right_basis[0], weight,
    )
    return outs[0][None], outs[1][None], outs[2][None], outs[3][None], outs[4]


def solution(mesh):
    owned = P(("dp", "tensor"), "pre", None)
    placed = P(None, "pre", "tensor")
    return jax.shard_map(
        local,
        mesh=mesh,
        in_specs=(P("dp", None, "pre", "tensor"), P(), owned, owned, owned, owned, owned, owned, placed),
        out_specs=(owned, owned, owned, owned, placed),
        check_vma=False,
    )
```

time: 438 us -> 132 us (0.30)
  the two profiles are of different devices: /device:TPU:8 before, /device:TPU:69 now
where the time goes in v1:
time: 132 us
  Pallas kernels  119 us (90%)
  local copies, waits for them, and re-layouts  11.9 us (9%)
    pallas_call x1, Pallas kernels, local(): pl.pallas_call(kernel, out_shape=[factor] * 4 + [jax.ShapeDtypeStruct((32...  119 us
    unnamed x23, local copies, waits for them, and re-layouts  11.9 us

profile of v1, /device:TPU:69, one launch (start us, length us, event | category | flops | bytes accessed | tf_op | source)
XLA Modules:
  0.0 131.8 jit_solution(3669374327535298885)
XLA Ops:
  0.6 0.0 copy-start.8
  0.6 0.6 copy-done.8
  1.3 0.0 copy-start
  1.3 1.0 copy-done
  2.3 0.0 copy-start.1
  2.3 1.0 copy-done.1
  3.4 0.0 copy-start.2
  3.4 0.9 copy-done.2
  4.3 0.0 copy-start.3
  4.3 0.9 copy-done.3
  5.3 0.0 copy-start.4
  5.3 0.9 copy-done.4
  6.2 0.0 copy-start.5
  6.2 0.9 copy-done.5
  7.2 0.0 copy-start.6
  7.2 0.9 copy-done.6
  8.1 0.0 copy-start.7
  8.1 0.9 copy-done.7
  9.0 119.2 %soap.1 = (f32[64,1024]{1,0:T(8,128)S(1)}, f32[64,1024]{1,0:T(8,128)S(1)}, f32[64,1024]{1,0:T(8,128)S(1)}, f32[64,1024]{1,0:T(8,128)S(1)}, bf16[32,64,128]{2,1,0:T(8,128)(2,1)S(1)}) custom-call(s32[32]{0:T(128)S(1)} %copy-done.8, bf16[32,64,128]{2,1,0:T(8,128)(2,1)S(1)} %bitcast.11, f32[64,1024]{1,0:T(8,128)S(1)} %bitcast.12, f32[64,1024]{1,0:T(8,128)S(1)} %bitcast.13, ...), custom_call_target="tpu_custom_call" | custom-call | tf_op jit(solution)/shard_map/soap/pallas_call | solution.py:303
  128.2 0.7 copy.19
  128.9 0.7 copy.20
  129.6 0.7 copy.21
  130.3 0.7 copy.22
  131.0 0.8 copy.23
Async XLA Ops:
  0.6 0.7 copy-start.8
  1.3 1.0 copy-start
  2.3 1.0 copy-start.1
  3.4 0.9 copy-start.2
  4.3 0.9 copy-start.3
  5.3 0.9 copy-start.4
  6.2 0.9 copy-start.5
  7.2 0.9 copy-start.6
  8.1 0.9 copy-start.7

commit v2 on v1

v2 whole, which is shorter than its diff:
```python
import jax
import jax.numpy as jnp
from jax import lax
from jax.experimental import pallas as pl
from jax.experimental.pallas import tpu as pltpu
from jax.sharding import PartitionSpec as P

factor_decay = 0.95
first_decay = 0.95
second_decay = 0.95
first_fix = 1.0 - (0.95**10) ** 10
second_fix = 1.0 - (0.95**10) ** 10
epsilon = 1e-08
weight_decay = 0.1

MESH = pl.DeviceIdType.MESH
F32 = jnp.float32
BF16 = jnp.bfloat16


def towards(zl, plane, parity):
    key = 2 * (zl - plane) + 2 * parity - 1
    return 2 * ((key + 16) // 16) - 1


def dot(a, b, dims=((1,), (0,))):
    return lax.dot_general(a, b, (dims, ((), ())), preferred_element_type=F32)


def kernel(
    slot, grad_in, left_in, right_in, first_in, second_in, basis_left, basis_right, weight_in,
    left_out, right_out, first_out, second_out, update_out,
    grad, left_old, right_old, first_old, second_old, weight, left_new, right_new, first_new, second_new, update,
    ins, outs,
    stage, rin, acc, gin, ghalf, qlh, qr, gfull, gturn, pbuf, prow, rot, rotb, rotr, firstb, secondb, firstr, secondr, cbuf, cnt, unrot,
    land, inv, s1s, s1r, s2s, s2r, lts, ltr, lps, lpr, lys, lyr, rts, rtr, rps, rpr, rys, ryr, qxs, qxr, mts, mtr,
    xts, xtr, gramb, gramr, gts, gtr, gps, gpr, gys, gyr, gxs, gxr, prs, prr, cs, cr_, us, uf, ur,
):
    k, t, p = lax.axis_index("dp"), lax.axis_index("tensor"), lax.axis_index("pre")
    x, co, zl, y = t // 2, t % 2, p // 4, p % 4
    half = zl // 2
    tr = ((y - x + 4) % 4) * 2 + zl % 2
    seat = (zl % 2) * 4 + y
    up, down, opposite = (y + 1) % 4, (y + 3) % 4, (y + 2) % 4
    twin = (k, x * 2 + half, (2 * co + zl % 2) * 4 + y)
    row = (2 * co + zl % 2) * 4 + y
    pair = (k, t, (zl + 1 - 2 * (zl % 2)) * 4 + y)
    other = (k, x * 2 + 1 - co, p)
    sent = []

    def group(core, place):
        return (k, x * 2 + core, (2 * half + place // 4) * 4 + place % 4)

    def root(xx, c):
        return (xx * 2 + half, (2 * c + co) * 4 + (x + xx) % 4)

    def push(src, dst, ssem, rsem, dev, here=None):
        copy = pltpu.make_async_remote_copy(
            src_ref=src, dst_ref=dst, send_sem=ssem, recv_sem=rsem, device_id=dev, device_id_type=MESH
        )
        if here is None:
            copy.start()
            sent.append((copy, None))
        else:
            away = jnp.logical_not(here)
            pl.when(away)(copy.start)
            pl.when(here)(pltpu.make_async_copy(src, dst, rsem).start)
            sent.append((copy, away))

    def arrived(dst, rsem):
        pltpu.make_async_copy(dst, dst, rsem).wait()

    loads = [
        pltpu.make_async_copy(src, dst, ins.at[i])
        for i, (src, dst) in enumerate(
            [(grad_in, grad), (first_in, first_old), (second_in, second_old), (left_in, left_old),
             (right_in, right_old), (weight_in, weight)]
        )
    ]
    for load in loads:
        load.start()
    stores = [
        pltpu.make_async_copy(src, dst, outs.at[i])
        for i, (src, dst) in enumerate(
            [(first_new, first_out), (second_new, second_out), (left_new, left_out), (right_new, right_out),
             (update, update_out)]
        )
    ]

    barrier = pltpu.get_barrier_semaphore()
    met = 0

    def greet(dev, here=None):
        def call():
            pl.semaphore_signal(barrier, inc=1, device_id=dev, device_id_type=MESH)

        if here is None:
            call()
        else:
            pl.when(jnp.logical_not(here))(call)
        return 1 if here is None else jnp.where(here, 0, 1)

    signs = [towards(zl, 2 * c + co, co) for c in range(2)]
    for step in (1, 3):
        met += greet(((k + step) % 4, t, p))
    for tt in range(8):
        for hh in range(2):
            met += greet(group(hh, tt), (hh == co) & (tt == seat))
    met += greet(twin, half == co)
    for q in range(8):
        there = co * 8 + q
        s = towards(2 * co + q // 4, zl, tr % 2)
        met += greet((k, tr, there), (tr == t) & (there == p))
        met += greet(((k - s + 4) % 4, tr, there))
    for c in range(2):
        for xx in range(4):
            there = root(xx, c)
            met += greet((k, *there), (there[0] == t) & (there[1] == p))
            met += greet(((k + signs[c] + 4) % 4, *there))

    loads[0].wait()
    for o in range(32):
        stage[(o // 8) * 8 + (o % 2) * 4 + (o % 8) // 2] = grad[slot[o]]
    loads[1].wait()
    loads[2].wait()
    firstb[...] = first_old[...].astype(BF16)
    secondb[...] = second_old[...].astype(BF16)
    slots = [slot[o] for o in range(32)]

    def invert(b, carry):
        total = jnp.int32(0)
        for o in range(32):
            place = (o // 8) * 8 + (o % 2) * 4 + (o % 8) // 2
            total = jnp.where(slots[o] == b, jnp.int32(place), total)
        inv[b] = total
        return carry

    lax.fori_loop(0, 32, invert, 0)
    pl.semaphore_wait(barrier, met)
    for c in range(2):
        s = signs[c]
        d1, d2 = (k - s + 4) % 4, (k + 2) % 4
        push(stage.at[pl.ds(d1 * 8 + c * 4, 4)], rin.at[c, 0], s1s.at[c * 2], s1r.at[c * 2], (d1, t, p))
        push(
            stage.at[pl.ds(d2 * 8 + c * 4, 4)], rin.at[c, 1], s1s.at[c * 2 + 1], s1r.at[c * 2 + 1],
            ((k + s + 4) % 4, t, p),
        )

    def lrows(j, yy):
        return qlh.at[pl.ds((j * 4 + yy) * 64, 64)]

    def rrows(j, yy):
        return qr.at[pl.ds(((2 * co + j) * 4 + yy) * 64, 64)]

    own_rows = pl.ds(p * 64, 64)
    mine, pairs = zl % 2, 1 - zl % 2
    push(basis_left, qlh.at[pl.ds((p % 8) * 64, 64)], lts, ltr, twin, half == co)
    push(basis_right, qr.at[own_rows], rts, rtr, twin, half == co)

    def along_y(rows, j, slot_j, ss, rs):
        push(rows(j, y), rows(j, y), ss.at[slot_j * 3], rs.at[j * 3], (k, t, zl * 4 + up))
        push(rows(j, y), rows(j, y), ss.at[slot_j * 3 + 1], rs.at[j * 3 + 1], (k, t, zl * 4 + down))

    def from_pair(rows, pr_, ss, rs):
        arrived(rows(pairs, y), pr_)
        along_y(rows, pairs, 1, ss, rs)

    def from_twin(rows, tr_, ps, pr_, ss, rs):
        arrived(rows(mine, y), tr_)
        push(rows(mine, y), rows(mine, y), ps, pr_, pair)
        along_y(rows, mine, 0, ss, rs)

    def relay(rows, ss, rs):
        arrived(rows(0, down), rs.at[0])
        push(rows(0, down), rows(0, down), ss.at[6], rs.at[2], (k, t, zl * 4 + up))
        arrived(rows(1, up), rs.at[4])
        push(rows(1, up), rows(1, up), ss.at[7], rs.at[5], (k, t, zl * 4 + down))

    def rest(rows, rs):
        arrived(rows(1, down), rs.at[3])
        arrived(rows(0, up), rs.at[1])

    def last(rows, rs):
        arrived(rows(0, opposite), rs.at[2])
        arrived(rows(1, opposite), rs.at[5])

    def across(places):
        for j, yy, at in places:
            push(rrows(j, yy), rrows(j, yy), qxs.at[at], qxr.at[j * 4 + yy], other)

    from_twin(lrows, ltr, lps, lpr, lys, lyr)
    from_twin(rrows, rtr, rps, rpr, rys, ryr)
    from_pair(lrows, lpr, lys, lyr)
    from_pair(rrows, rpr, rys, ryr)

    for c in range(2):
        s = signs[c]
        for way in range(2):
            arrived(rin.at[c, way], s1r.at[c * 2 + way])
            owner = k if way == 0 else (k + s + 4) % 4
            own = stage[pl.ds(owner * 8 + c * 4, 4)]
            acc[c, way] = (own.astype(F32) + rin[c, way].astype(F32)).astype(BF16)
            for xx in range(4):
                place = (owner, *root(xx, c))
                here = None
                if way == 0:
                    here = (place[1] == t) & (place[2] == p)
                push(
                    acc.at[c, way, xx], gin.at[way, p % 8], s2s.at[c * 8 + way * 4 + xx], s2r.at[way * 8 + p % 8],
                    place, here,
                )

    push(firstb, firstr, mts.at[0], mtr.at[0], twin, half == co)
    push(secondb, secondr, mts.at[1], mtr.at[1], twin, half == co)
    relay(lrows, lys, lyr)
    relay(rrows, rys, ryr)
    across([(0, y, 0), (1, y, 1), (0, down, 2), (1, up, 3)])

    for q in range(8):
        for way in range(2):
            arrived(gin.at[way, q], s2r.at[way * 8 + q])
        ghalf[pl.ds(q * 64, 64)] = (gin[0, q].astype(F32) + gin[1, q].astype(F32)).astype(BF16)

    rest(lrows, lyr)
    last(lrows, lyr)

    gt = ghalf[...].astype(F32).T.astype(BF16)
    for n in range(4):
        turned = dot(gt, qlh[:, pl.ds(n * 256, 256)])
        pbuf[pl.ds(n * 256, 256)] = turned.T.astype(BF16)
        for there in range(n * 4, n * 4 + 4):
            push(
                pbuf.at[pl.ds(there * 64, 64)], prow.at[co, :, pl.ds(pl.multiple_of(tr * 128, 128), 128)],
                prs.at[there], prr.at[co * 8 + tr], group(there // 8, (there // 4) % 2 * 4 + there % 4), there == row,
            )
    def gpart(j, yy):
        column = ((yy - x + 4) % 4) * 2 + j
        return gfull.at[pl.ds(co * 512, 512), pl.ds(pl.multiple_of(column * 128, 128), 128)]

    def gacross(places):
        for j, yy, at in places:
            push(gpart(j, yy), gpart(j, yy), gxs.at[at], gxr.at[j * 4 + yy], other)

    gfull[pl.ds(co * 512, 512), pl.ds(pl.multiple_of(tr * 128, 128), 128)] = ghalf[...]
    push(gpart(mine, y), gpart(mine, y), gps, gpr, pair)
    along_y(gpart, mine, 0, gys, gyr)

    rest(rrows, ryr)
    across([(1, down, 4), (0, up, 5)])
    last(rrows, ryr)
    across([(0, opposite, 6), (1, opposite, 7)])
    for i in range(8):
        arrived(qr.at[pl.ds(((1 - co) * 8 + i) * 64, 64)], qxr.at[i])
    for i, ref in enumerate((firstr, secondr)):
        arrived(ref, mtr.at[i])

    for hh in range(2):
        for tt in range(8):
            arrived(prow.at[hh, :, pl.ds(tt * 128, 128)], prr.at[hh * 8 + tt])
    projected = (prow[0].astype(F32) + prow[1].astype(F32)).astype(BF16)
    for n in range(4):
        lanes = pl.ds(n * 256, 256)
        rotated = dot(projected, qr[:, lanes])
        rotb[:, lanes] = rotated.astype(BF16)
        first_next = first_decay * firstr[:, lanes].astype(F32) + (1.0 - first_decay) * rotated
        second_next = second_decay * secondr[:, lanes].astype(F32) + (1.0 - second_decay) * rotated * rotated
        rot[:, lanes] = (first_next / first_fix / (jnp.sqrt(second_next / second_fix) + epsilon)).astype(BF16)
    for n in range(4):
        cbuf[:, pl.ds(n * 256, 256)] = dot(rot[...], qr[pl.ds(n * 256, 256), :], ((1,), (1,))).astype(BF16)
        for tt in (2 * n, 2 * n + 1):
            for hh in range(2):
                push(
                    cbuf.at[:, pl.ds(tt * 128, 128)], cnt.at[pl.ds(row * 64, 64)], cs.at[hh * 8 + tt], cr_.at[row],
                    group(hh, tt % 2 * 4 + (tt // 2 + x) % 4), (hh == co) & (tr == tt),
                )
    push(rotb, rotr, xts, xtr, twin, half == co)

    from_pair(gpart, gpr, gys, gyr)
    gacross([(0, y, 0), (1, y, 1)])

    for q in range(16):
        arrived(cnt.at[pl.ds(q * 64, 64)], cr_.at[q])
    for n in range(2):
        unrot[pl.ds(n * 256, 256)] = dot(qlh[pl.ds(n * 256, 256), :], cnt[...]).astype(BF16)
        for q in range(n * 4, n * 4 + 4):
            s = towards(2 * co + q // 4, zl, tr % 2)
            index = k * 8 + half * 4 + x
            there = co * 8 + q
            push(
                unrot.at[pl.ds(q * 64, 64)], land.at[index], us.at[q * 2], ur.at[index], (k, tr, there),
                here=(tr == t) & (there == p),
            )
            push(
                unrot.at[pl.ds(q * 64, 64)], land.at[index], us.at[q * 2 + 1], ur.at[index],
                ((k - s + 4) % 4, tr, there),
            )

    relay(gpart, gys, gyr)
    gacross([(0, down, 2), (1, up, 3)])
    rest(gpart, gyr)
    gacross([(1, down, 4), (0, up, 5)])

    arrived(rotr, xtr)
    for n in range(4):
        lanes = pl.ds(n * 256, 256)
        rotated = rotr[:, lanes].astype(F32)
        first_new[:, lanes] = first_decay * first_old[:, lanes] + (1.0 - first_decay) * rotated
        second_new[:, lanes] = second_decay * second_old[:, lanes] + (1.0 - second_decay) * rotated * rotated
    stores[0].start()
    stores[1].start()

    for c in range(2):
        s = signs[c]
        for xx in range(4):
            one, two = k * 8 + c * 4 + xx, ((k + s + 4) % 4) * 8 + c * 4 + xx
            arrived(land.at[one], ur.at[one])
            push(land.at[one], land.at[one], uf.at[c * 8 + xx], ur.at[one], ((k + s + 4) % 4, t, p))
            arrived(land.at[two], ur.at[two])
            push(land.at[two], land.at[two], uf.at[c * 8 + 4 + xx], ur.at[two], ((k - s + 4) % 4, t, p))

    last(gpart, gyr)
    gacross([(0, opposite, 6), (1, opposite, 7)])
    for i in range(8):
        arrived(gfull.at[pl.ds((1 - co) * 512, 512), pl.ds(0, 128)], gxr.at[i])
    for n in range(4):
        lanes = pl.ds(n * 256, 256)
        gramb[0, :, lanes] = dot(gfull[pl.ds(row * 64, 64), :], gfull[lanes, :], ((1,), (1,))).astype(BF16)
    push(gramb.at[0], gramr.at[0], gts.at[0], gtr.at[0], twin, half == co)
    gcols = gfull[:, pl.ds(pl.multiple_of((row // 2) * 128, 128), 128)]
    gturn[...] = gcols.astype(F32).T.astype(BF16)
    for n in range(4):
        lanes = pl.ds(n * 256, 256)
        gramb[1, :, lanes] = dot(gturn[pl.ds((row % 2) * 64, 64), :], gfull[:, lanes]).astype(BF16)
    push(gramb.at[1], gramr.at[1], gts.at[1], gtr.at[1], twin, half == co)
    loads[3].wait()
    loads[4].wait()
    loads[5].wait()
    for i, (old, new) in enumerate(((left_old, left_new), (right_old, right_new))):
        arrived(gramr.at[i], gtr.at[i])
        new[...] = factor_decay * old[...] + (1.0 - factor_decay) * gramr[i].astype(F32)
        stores[2 + i].start()

    for c in range(2):
        s = signs[c]
        for xx in range(4):
            three, four = ((k - s + 4) % 4) * 8 + c * 4 + xx, ((k + 2) % 4) * 8 + c * 4 + xx
            arrived(land.at[three], ur.at[three])
            arrived(land.at[four], ur.at[four])

    for b in range(32):
        update[b] = (land[inv[b]].astype(F32) + weight_decay * weight[b].astype(F32)).astype(BF16)

    stores[4].start()
    for copy, away in sent:
        if away is None:
            copy.wait_send()
        else:
            pl.when(away)(copy.wait_send)
    for store in stores:
        store.wait()


def local(
    grad_parts, slot_block, left_factor, right_factor, first_moment, second_moment, left_basis, right_basis, weight
):
    anywhere = pl.BlockSpec(memory_space=pltpu.HBM)
    dma = lambda n: pltpu.SemaphoreType.DMA((n,))
    one = pltpu.SemaphoreType.DMA
    factor = jax.ShapeDtypeStruct((64, 1024), F32)
    outs = pl.pallas_call(
        kernel,
        out_shape=[factor] * 4 + [jax.ShapeDtypeStruct((32, 64, 128), BF16)],
        in_specs=[pl.BlockSpec(memory_space=pltpu.SMEM)] + [anywhere] * 8,
        out_specs=[anywhere] * 5,
        scratch_shapes=[
            pltpu.VMEM((32, 64, 128), BF16),
            *[pltpu.VMEM((64, 1024), F32)] * 4,
            pltpu.VMEM((32, 64, 128), BF16),
            *[pltpu.VMEM((64, 1024), F32)] * 4,
            pltpu.VMEM((32, 64, 128), BF16),
            dma(6), dma(5),
            pltpu.VMEM((32, 64, 128), BF16),
            pltpu.VMEM((2, 2, 4, 64, 128), BF16),
            pltpu.VMEM((2, 2, 4, 64, 128), BF16),
            pltpu.VMEM((2, 8, 64, 128), BF16),
            pltpu.VMEM((512, 128), BF16),
            pltpu.VMEM((512, 1024), BF16),
            pltpu.VMEM((1024, 1024), BF16),
            pltpu.VMEM((1024, 1024), BF16),
            pltpu.VMEM((128, 1024), BF16),
            pltpu.VMEM((1024, 128), BF16),
            pltpu.VMEM((2, 64, 1024), BF16),
            *[pltpu.VMEM((64, 1024), BF16)] * 8,
            pltpu.VMEM((1024, 128), BF16),
            pltpu.VMEM((512, 128), BF16),
            pltpu.VMEM((32, 64, 128), BF16),
            pltpu.SMEM((32,), jnp.int32),
            dma(4), dma(4), dma(16), dma(16),
            one, one, one, one, dma(8), dma(6),
            one, one, one, one, dma(8), dma(6),
            dma(8), dma(8), dma(2), dma(2), one, one,
            *[pltpu.VMEM((2, 64, 1024), BF16)] * 2,
            dma(2), dma(2), one, one, dma(8), dma(6), dma(8), dma(8),
            dma(16), dma(16), dma(16), dma(16),
            dma(16), dma(16), dma(32),
        ],
        compiler_params=pltpu.CompilerParams(collective_id=0, has_side_effects=True, vmem_limit_bytes=63 * 1024 * 1024),
        name="soap",
    )(
        slot_block, grad_parts[0], left_factor[0], right_factor[0], first_moment[0], second_moment[0],
        left_basis[0], right_basis[0], weight,
    )
    return outs[0][None], outs[1][None], outs[2][None], outs[3][None], outs[4]


def solution(mesh):
    owned = P(("dp", "tensor"), "pre", None)
    placed = P(None, "pre", "tensor")
    return jax.shard_map(
        local,
        mesh=mesh,
        in_specs=(P("dp", None, "pre", "tensor"), P(), owned, owned, owned, owned, owned, owned, placed),
        out_specs=(owned, owned, owned, owned, placed),
        check_vma=False,
    )
```

time: 132 us -> 99.8 us (0.76)
  the two profiles are of different devices: /device:TPU:69 before, /device:TPU:3 now
where the time goes in v2:
time: 99.8 us; the launch traced here: 99.6 us
  Pallas kernels  94 us (94%)
  local copies, waits for them, and re-layouts  4.96 us (5%)
    pallas_call x1, Pallas kernels, local(): pl.pallas_call(kernel, out_shape=[factor] * 4 + [jax.ShapeDtypeStruct((32...  94 us
    unnamed x13, local copies, waits for them, and re-layouts  4.96 us

profile of v2, /device:TPU:3, one launch (start us, length us, event | category | flops | bytes accessed | tf_op | source)
XLA Modules:
  0.0 99.6 jit_solution(12388617841581391031)
XLA Ops:
  0.6 94.0 %soap.1 = (f32[64,1024]{1,0:T(8,128)}, f32[64,1024]{1,0:T(8,128)}, f32[64,1024]{1,0:T(8,128)}, f32[64,1024]{1,0:T(8,128)}, bf16[32,64,128]{2,1,0:T(8,128)(2,1)}) custom-call(s32[32]{0:T(128)} %slot.1, bf16[32,64,128]{2,1,0:T(8,128)(2,1)} %bitcast.11, f32[64,1024]{1,0:T(8,128)} %bitcast.12, f32[64,1024]{1,0:T(8,128)} %bitcast.13, f32[64,1024]{1,0:T(8,128)} %bitcast.14, ...), custom_call_target="tpu_custom_call" | custom-call | tf_op jit(solution)/shard_map/soap/pallas_call | solution.py:370
  94.6 0.0 copy-start.3
  94.6 1.7 %copy.19 = f32[1,64,1024]{2,1,0:T(8,128)} copy(f32[1,64,1024]{2,1,0:T(8,128)} %bitcast.19) | data formatting | bytes 524288
  96.3 0.0 copy-done.3
  96.3 0.0 copy-start.2
  96.3 0.0 copy-start.1
  96.3 0.7 copy.20
  97.0 0.3 copy-done.2
  97.4 0.0 copy-start
  97.4 0.7 copy.21
  98.1 0.0 copy-done.1
  98.1 0.7 copy.22
  98.8 0.0 copy-done
  98.8 0.8 copy.23
Async XLA Ops:
  94.6 1.7 %copy-start.3 = (f32[64,1024]{1,0:T(8,128)S(1)}, f32[64,1024]{1,0:T(8,128)}, u32[]{:S(2)}) copy-start(f32[64,1024]{1,0:T(8,128)} %get-tuple-element.11) | copy-start | bytes 786436
  96.3 1.0 %copy-start.2 = (f32[64,1024]{1,0:T(8,128)S(1)}, f32[64,1024]{1,0:T(8,128)}, u32[]{:S(2)}) copy-start(f32[64,1024]{1,0:T(8,128)} %get-tuple-element.12) | copy-start | bytes 786436
  96.3 1.8 %copy-start.1 = (f32[64,1024]{1,0:T(8,128)S(1)}, f32[64,1024]{1,0:T(8,128)}, u32[]{:S(2)}) copy-start(f32[64,1024]{1,0:T(8,128)} %get-tuple-element.13) | copy-start | bytes 786436
  97.4 1.4 %copy-start = (bf16[32,64,128]{2,1,0:T(8,128)(2,1)S(1)}, bf16[32,64,128]{2,1,0:T(8,128)(2,1)}, u32[]{:S(2)}) copy-start(bf16[32,64,128]{2,1,0:T(8,128)(2,1)} %get-tuple-element.24) | copy-start | bytes 1572868

commit v3 on v2

--- a/solution.py
+++ b/solution.py
@@ -101,22 +101,22 @@
         return 1 if here is None else jnp.where(here, 0, 1)
 
     signs = [towards(zl, 2 * c + co, co) for c in range(2)]
+    for q in range(8):
+        there = co * 8 + q
+        s = towards(2 * co + q // 4, zl, tr % 2)
+        met += greet((k, tr, there), (tr == t) & (there == p))
+        met += greet(((k - s + 4) % 4, tr, there))
+    for c in range(2):
+        for xx in range(4):
+            there = root(xx, c)
+            met += greet((k, *there), (there[0] == t) & (there[1] == p))
+            met += greet(((k + signs[c] + 4) % 4, *there))
     for step in (1, 3):
         met += greet(((k + step) % 4, t, p))
     for tt in range(8):
         for hh in range(2):
             met += greet(group(hh, tt), (hh == co) & (tt == seat))
     met += greet(twin, half == co)
-    for q in range(8):
-        there = co * 8 + q
-        s = towards(2 * co + q // 4, zl, tr % 2)
-        met += greet((k, tr, there), (tr == t) & (there == p))
-        met += greet(((k - s + 4) % 4, tr, there))
-    for c in range(2):
-        for xx in range(4):
-            there = root(xx, c)
-            met += greet((k, *there), (there[0] == t) & (there[1] == p))
-            met += greet(((k + signs[c] + 4) % 4, *there))
 
     loads[0].wait()
     for o in range(32):
@@ -137,14 +137,15 @@
 
     lax.fori_loop(0, 32, invert, 0)
     pl.semaphore_wait(barrier, met)
+    own_rows = pl.ds(p * 64, 64)
+    push(basis_left, qlh.at[pl.ds((p % 8) * 64, 64)], lts, ltr, twin, half == co)
+    push(basis_right, qr.at[own_rows], rts, rtr, twin, half == co)
     for c in range(2):
         s = signs[c]
-        d1, d2 = (k - s + 4) % 4, (k + 2) % 4
-        push(stage.at[pl.ds(d1 * 8 + c * 4, 4)], rin.at[c, 0], s1s.at[c * 2], s1r.at[c * 2], (d1, t, p))
-        push(
-            stage.at[pl.ds(d2 * 8 + c * 4, 4)], rin.at[c, 1], s1s.at[c * 2 + 1], s1r.at[c * 2 + 1],
-            ((k + s + 4) % 4, t, p),
-        )
+        for xx in range(4):
+            for way, owner, there in ((0, (k - s + 4) % 4, (k - s + 4) % 4), (1, (k + 2) % 4, (k + s + 4) % 4)):
+                at = c * 8 + way * 4 + xx
+                push(stage.at[owner * 8 + c * 4 + xx], rin.at[c, way, xx], s1s.at[at], s1r.at[at], (there, t, p))
 
     def lrows(j, yy):
         return qlh.at[pl.ds((j * 4 + yy) * 64, 64)]
@@ -154,8 +155,6 @@
 
     own_rows = pl.ds(p * 64, 64)
     mine, pairs = zl % 2, 1 - zl % 2
-    push(basis_left, qlh.at[pl.ds((p % 8) * 64, 64)], lts, ltr, twin, half == co)
-    push(basis_right, qr.at[own_rows], rts, rtr, twin, half == co)
 
     def along_y(rows, j, slot_j, ss, rs):
         push(rows(j, y), rows(j, y), ss.at[slot_j * 3], rs.at[j * 3], (k, t, zl * 4 + up))
@@ -195,20 +194,16 @@
 
     for c in range(2):
         s = signs[c]
-        for way in range(2):
-            arrived(rin.at[c, way], s1r.at[c * 2 + way])
-            owner = k if way == 0 else (k + s + 4) % 4
-            own = stage[pl.ds(owner * 8 + c * 4, 4)]
-            acc[c, way] = (own.astype(F32) + rin[c, way].astype(F32)).astype(BF16)
-            for xx in range(4):
+        for xx in range(4):
+            for way in range(2):
+                at = c * 8 + way * 4 + xx
+                arrived(rin.at[c, way, xx], s1r.at[at])
+                owner = k if way == 0 else (k + s + 4) % 4
+                own = stage[owner * 8 + c * 4 + xx]
+                acc[c, way, xx] = (own.astype(F32) + rin[c, way, xx].astype(F32)).astype(BF16)
                 place = (owner, *root(xx, c))
-                here = None
-                if way == 0:
-                    here = (place[1] == t) & (place[2] == p)
-                push(
-                    acc.at[c, way, xx], gin.at[way, p % 8], s2s.at[c * 8 + way * 4 + xx], s2r.at[way * 8 + p % 8],
-                    place, here,
-                )
+                here = (place[1] == t) & (place[2] == p) if way == 0 else None
+                push(acc.at[c, way, xx], gin.at[way, p % 8], s2s.at[at], s2r.at[way * 8 + p % 8], place, here)
 
     push(firstb, firstr, mts.at[0], mtr.at[0], twin, half == co)
     push(secondb, secondr, mts.at[1], mtr.at[1], twin, half == co)
@@ -312,9 +307,13 @@
     for c in range(2):
         s = signs[c]
         for xx in range(4):
-            one, two = k * 8 + c * 4 + xx, ((k + s + 4) % 4) * 8 + c * 4 + xx
+            one = k * 8 + c * 4 + xx
             arrived(land.at[one], ur.at[one])
             push(land.at[one], land.at[one], uf.at[c * 8 + xx], ur.at[one], ((k + s + 4) % 4, t, p))
+    for c in range(2):
+        s = signs[c]
+        for xx in range(4):
+            two = ((k + s + 4) % 4) * 8 + c * 4 + xx
             arrived(land.at[two], ur.at[two])
             push(land.at[two], land.at[two], uf.at[c * 8 + 4 + xx], ur.at[two], ((k - s + 4) % 4, t, p))
 
@@ -358,6 +357,19 @@
             pl.when(away)(copy.wait_send)
     for store in stores:
         store.wait()
+
+
+def hand_over(*refs):
+    given, taken, held, ins, outs = refs[:5], refs[5:10], refs[10:15], refs[15], refs[16]
+    reads = [pltpu.make_async_copy(given[i], held[i], ins.at[i]) for i in range(5)]
+    writes = [pltpu.make_async_copy(held[i], taken[i], outs.at[i]) for i in range(5)]
+    for read in reads:
+        read.start()
+    for read, write in zip(reads, writes):
+        read.wait()
+        write.start()
+    for write in writes:
+        write.wait()
 
 
 def local(
@@ -395,7 +407,7 @@
             pltpu.VMEM((512, 128), BF16),
             pltpu.VMEM((32, 64, 128), BF16),
             pltpu.SMEM((32,), jnp.int32),
-            dma(4), dma(4), dma(16), dma(16),
+            dma(16), dma(16), dma(16), dma(16),
             one, one, one, one, dma(8), dma(6),
             one, one, one, one, dma(8), dma(6),
             dma(8), dma(8), dma(2), dma(2), one, one,
@@ -410,6 +422,15 @@
         slot_block, grad_parts[0], left_factor[0], right_factor[0], first_moment[0], second_moment[0],
         left_basis[0], right_basis[0], weight,
     )
+    outs = pl.pallas_call(
+        hand_over,
+        out_shape=[factor] * 4 + [jax.ShapeDtypeStruct((32, 64, 128), BF16)],
+        in_specs=[anywhere] * 5,
+        out_specs=[anywhere] * 5,
+        scratch_shapes=[*[pltpu.VMEM((64, 1024), F32)] * 4, pltpu.VMEM((32, 64, 128), BF16), dma(5), dma(5)],
+        compiler_params=pltpu.CompilerParams(vmem_limit_bytes=63 * 1024 * 1024),
+        name="hand_over",
+    )(*outs)
     return outs[0][None], outs[1][None], outs[2][None], outs[3][None], outs[4]
 
 

time: 99.8 us -> 96.3 us (0.965)
  the two profiles are of different devices: /device:TPU:3 before, /device:TPU:191 now
where the time goes in v3:
time: 96.3 us; the launch traced here: 96.1 us
  Pallas kernels  95.4 us (99%)
    pallas_call x1, Pallas kernels, local(): pl.pallas_call(kernel, out_shape=[factor] * 4 + [jax.ShapeDtypeStruct((32...  93.2 us
    pallas_call x1, Pallas kernels, local(): pl.pallas_call(hand_over, out_shape=[factor] * 4 + [jax.ShapeDtypeStruct(...  2.24 us

profile of v3, /device:TPU:191, one launch (start us, length us, event | category | flops | bytes accessed | tf_op | source)
XLA Modules:
  0.0 96.1 jit_solution(7747331363899716865)
XLA Ops:
  0.6 93.2 %soap.1 = (f32[64,1024]{1,0:T(8,128)}, f32[64,1024]{1,0:T(8,128)}, f32[64,1024]{1,0:T(8,128)}, f32[64,1024]{1,0:T(8,128)}, bf16[32,64,128]{2,1,0:T(8,128)(2,1)}) custom-call(s32[32]{0:T(128)} %slot.1, bf16[32,64,128]{2,1,0:T(8,128)(2,1)} %bitcast.11, f32[64,1024]{1,0:T(8,128)} %bitcast.12, f32[64,1024]{1,0:T(8,128)} %bitcast.13, f32[64,1024]{1,0:T(8,128)} %bitcast.14, ...), custom_call_target="tpu_custom_call" | custom-call | tf_op jit(solution)/shard_map/soap/pallas_call | solution.py:382
  93.8 2.2 %hand_over.1 = (f32[64,1024]{1,0:T(8,128)}, f32[64,1024]{1,0:T(8,128)}, f32[64,1024]{1,0:T(8,128)}, f32[64,1024]{1,0:T(8,128)}, bf16[32,64,128]{2,1,0:T(8,128)(2,1)}) custom-call(f32[64,1024]{1,0:T(8,128)} %get-tuple-element.15.refs_0_, f32[64,1024]{1,0:T(8,128)} %get-tuple-element.16.refs_1_, f32[64,1024]{1,0:T(8,128)} %get-tuple-element.17.refs_2_, ...), custom_call_target="tpu_custom_call" | custom-call | tf_op jit(solution)/shard_map/hand_over/pallas_call | solution.py:425

commit v4 on v3

--- a/solution.py
+++ b/solution.py
@@ -282,16 +282,30 @@
             index = k * 8 + half * 4 + x
             there = co * 8 + q
             push(
+                unrot.at[pl.ds(q * 64, 64)], land.at[index], us.at[q * 2 + 1], ur.at[index],
+                ((k - s + 4) % 4, tr, there),
+            )
+            push(
                 unrot.at[pl.ds(q * 64, 64)], land.at[index], us.at[q * 2], ur.at[index], (k, tr, there),
                 here=(tr == t) & (there == p),
             )
-            push(
-                unrot.at[pl.ds(q * 64, 64)], land.at[index], us.at[q * 2 + 1], ur.at[index],
-                ((k - s + 4) % 4, tr, there),
-            )
 
     relay(gpart, gys, gyr)
     gacross([(0, down, 2), (1, up, 3)])
+
+    for c in range(2):
+        s = signs[c]
+        for xx in range(4):
+            one = k * 8 + c * 4 + xx
+            arrived(land.at[one], ur.at[one])
+            push(land.at[one], land.at[one], uf.at[c * 8 + xx], ur.at[one], ((k + s + 4) % 4, t, p))
+    for c in range(2):
+        s = signs[c]
+        for xx in range(4):
+            two = ((k + s + 4) % 4) * 8 + c * 4 + xx
+            arrived(land.at[two], ur.at[two])
+            push(land.at[two], land.at[two], uf.at[c * 8 + 4 + xx], ur.at[two], ((k - s + 4) % 4, t, p))
+
     rest(gpart, gyr)
     gacross([(1, down, 4), (0, up, 5)])
 
@@ -303,19 +317,6 @@
         second_new[:, lanes] = second_decay * second_old[:, lanes] + (1.0 - second_decay) * rotated * rotated
     stores[0].start()
     stores[1].start()
-
-    for c in range(2):
-        s = signs[c]
-        for xx in range(4):
-            one = k * 8 + c * 4 + xx
-            arrived(land.at[one], ur.at[one])
-            push(land.at[one], land.at[one], uf.at[c * 8 + xx], ur.at[one], ((k + s + 4) % 4, t, p))
-    for c in range(2):
-        s = signs[c]
-        for xx in range(4):
-            two = ((k + s + 4) % 4) * 8 + c * 4 + xx
-            arrived(land.at[two], ur.at[two])
-            push(land.at[two], land.at[two], uf.at[c * 8 + 4 + xx], ur.at[two], ((k - s + 4) % 4, t, p))
 
     last(gpart, gyr)
     gacross([(0, opposite, 6), (1, opposite, 7)])

time: 96.3 us -> 96.4 us (level)
  no operation moved by 1% of the time
where the time goes in v4:
time: 96.4 us; the launch traced here: 96.2 us
  Pallas kernels  95.5 us (99%)
    pallas_call x1, Pallas kernels, local(): pl.pallas_call(kernel, out_shape=[factor] * 4 + [jax.ShapeDtypeStruct((32...  93.3 us
    pallas_call x1, Pallas kernels, local(): pl.pallas_call(hand_over, out_shape=[factor] * 4 + [jax.ShapeDtypeStruct(...  2.24 us

profile of v4, /device:TPU:191, one launch (start us, length us, event | category | flops | bytes accessed | tf_op | source)
XLA Modules:
  0.0 96.2 jit_solution(3268117587791271705)
XLA Ops:
  0.6 93.3 %soap.1 = (f32[64,1024]{1,0:T(8,128)}, f32[64,1024]{1,0:T(8,128)}, f32[64,1024]{1,0:T(8,128)}, f32[64,1024]{1,0:T(8,128)}, bf16[32,64,128]{2,1,0:T(8,128)(2,1)}) custom-call(s32[32]{0:T(128)} %slot.1, bf16[32,64,128]{2,1,0:T(8,128)(2,1)} %bitcast.11, f32[64,1024]{1,0:T(8,128)} %bitcast.12, f32[64,1024]{1,0:T(8,128)} %bitcast.13, f32[64,1024]{1,0:T(8,128)} %bitcast.14, ...), custom_call_target="tpu_custom_call" | custom-call | tf_op jit(solution)/shard_map/soap/pallas_call | solution.py:383
  93.9 2.2 %hand_over.1 = (f32[64,1024]{1,0:T(8,128)}, f32[64,1024]{1,0:T(8,128)}, f32[64,1024]{1,0:T(8,128)}, f32[64,1024]{1,0:T(8,128)}, bf16[32,64,128]{2,1,0:T(8,128)(2,1)}) custom-call(f32[64,1024]{1,0:T(8,128)} %get-tuple-element.15.refs_0_, f32[64,1024]{1,0:T(8,128)} %get-tuple-element.16.refs_1_, f32[64,1024]{1,0:T(8,128)} %get-tuple-element.17.refs_2_, ...), custom_call_target="tpu_custom_call" | custom-call | tf_op jit(solution)/shard_map/hand_over/pallas_call | solution.py:426
